TPU v7x, 32 devices: a whole 2x2x4 slice. The times are simulated.
32 devices in a mesh: groups: 2 (over y), seq: 8 (over z, core), fsdp: 2 (over x).
Axes of the slice: x: 2, y: 2, z: 4, core: 2. Of those that a mesh axis runs over, the one named last changes fastest.
Arguments:
- query_rows: bfloat16 [4096, 2048], P(('groups', 'seq'), 'fsdp'), parts along dimension 0, may hold values from -6 to 6
- key_rows: bfloat16 [4096, 2048], P(('groups', 'seq'), 'fsdp'), parts along dimension 0, may hold values from -6 to 6
- value_rows: bfloat16 [4096, 2048], P(('groups', 'seq'), 'fsdp'), parts along dimension 0, may hold values from -6 to 6
- out_weight: bfloat16 [2048, 2048], P('fsdp', 'seq'), may hold values from -0.125 to 0.125
- out_grad: bfloat16 [4096, 2048], P(('groups', 'seq')), parts along dimension 0, may hold values from -6 to 6
Outputs:
- mixed: bfloat16 [4096, 2048], P(('groups', 'seq')), parts along dimension 0
- query_grad: bfloat16 [4096, 2048], P(('groups', 'seq'), 'fsdp'), parts along dimension 0
- key_grad: bfloat16 [4096, 2048], P(('groups', 'seq'), 'fsdp'), parts along dimension 0
- value_grad: bfloat16 [4096, 2048], P(('groups', 'seq'), 'fsdp'), parts along dimension 0
- weight_grad: float32 [4096, 2048], P(('groups', 'fsdp'), 'seq'), parts along dimension 0
There are 2 independent parts, one for each index of `groups`. A program takes and returns all parts, laid end to end along the dimension named above; an argument that names none is the same for every part. Nothing has to cross between parts.
All inputs are finite; a program needn't handle non-finite values.
Results may differ from a plain program's by a relative error of at most 0.013.
Values may be sent and summed in bfloat16 or wider, within the bound.
A program may use at most 128 MiB of HBM per device.

v0:
```python
import math

import jax
import jax.numpy as jnp
from jax import lax
from jax.sharding import PartitionSpec as P

HD = 128


HIGH = lax.Precision.HIGHEST


def prefix_2(value, axis, join, neutral, backward):
    count = lax.axis_size(axis)
    place = lax.axis_index(axis)
    ahead = count - 1 - place if backward else place
    gathered = lax.all_gather(value.astype(jnp.bfloat16), axis)
    state = jnp.zeros_like(value) + jnp.asarray(neutral, value.dtype)

    def one(lap, state):
        source = count - 1 - lap if backward else lap
        return join(state, lax.dynamic_index_in_dim(gathered, source, 0, False).astype(value.dtype))

    return lax.fori_loop(0, ahead, one, state)


def added(earlier, later):
    return jax.tree.map(lambda first, second: first + second, earlier, later)


def on_device(query_rows, key_rows, value_rows, out_weight, out_grad):
    length = query_rows.shape[0]
    width = query_rows.shape[1]
    heads_here = width // HD
    total = length * lax.axis_size("seq")
    factor = 1.0 / math.sqrt(HD * total)
    grad_factor = 1.0 / math.sqrt(total)
    queries = query_rows.reshape(length, heads_here, HD)
    keys = key_rows.reshape(length, heads_here, HD)
    values = value_rows.reshape(length, heads_here, HD)
    full_weight = lax.all_gather(out_weight, "seq", axis=1, tiled=True)
    attn_grad = lax.dot_general(
        out_grad, full_weight, (((1,), (1,)), ((), ())), preferred_element_type=jnp.float32
    ).astype(jnp.bfloat16)
    grads = attn_grad.reshape(length, heads_here, HD)
    own_state = jnp.einsum("thd,the->hde", keys, values, preferred_element_type=jnp.float32)
    own_grad_state = jnp.einsum("thd,the->hde", queries, grads, preferred_element_type=jnp.float32)
    zeros = jnp.zeros_like(own_state)
    prefix = prefix_2(own_state, "seq", added, zeros, False)
    suffix = prefix_2(own_grad_state, "seq", added, zeros, True)
    positions = jnp.arange(length)
    causal = positions[:, None] >= positions[None, :]
    raw_scores = (
        jnp.einsum("thd,shd->hts", queries, keys, preferred_element_type=jnp.float32) * factor
    )
    scores = jnp.where(causal, raw_scores, 0.0).astype(jnp.bfloat16)
    within = jnp.einsum("hts,shd->thd", scores, values, preferred_element_type=jnp.float32)
    carried = (
        jnp.einsum("thd,hde->the", queries.astype(jnp.float32), prefix, precision=HIGH) * factor
    )
    attention = (within + carried).astype(jnp.bfloat16).reshape(length, width)
    partial_out = jnp.dot(attention, full_weight, preferred_element_type=jnp.float32)
    mixed = lax.psum(partial_out.astype(jnp.bfloat16), "fsdp")
    weight_grad = lax.psum_scatter(
        lax.dot_general(
            out_grad, attention, (((0,), (0,)), ((), ())), preferred_element_type=jnp.float32
        )
        * grad_factor,
        "seq",
        scatter_dimension=0,
        tiled=True,
    ).T
    raw_mixing = (
        jnp.einsum("the,she->hts", grads, values, preferred_element_type=jnp.float32) * factor
    )
    mixing = jnp.where(causal, raw_mixing, 0.0).astype(jnp.bfloat16)
    query_grad = jnp.einsum(
        "hts,shd->thd", mixing, keys, preferred_element_type=jnp.float32
    ) + factor * jnp.einsum("the,hde->thd", grads.astype(jnp.float32), prefix, precision=HIGH)
    key_grad = jnp.einsum(
        "hts,thd->shd", mixing, queries, preferred_element_type=jnp.float32
    ) + factor * jnp.einsum("the,hde->thd", values.astype(jnp.float32), suffix, precision=HIGH)
    value_grad = jnp.einsum(
        "hts,the->she", scores, grads, preferred_element_type=jnp.float32
    ) + factor * jnp.einsum("thd,hde->the", keys.astype(jnp.float32), suffix, precision=HIGH)
    query_grad = query_grad.astype(jnp.bfloat16).reshape(length, width)
    key_grad = key_grad.astype(jnp.bfloat16).reshape(length, width)
    value_grad = value_grad.astype(jnp.bfloat16).reshape(length, width)
    return (mixed, query_grad, key_grad, value_grad, weight_grad)


def solution(mesh):
    return jax.shard_map(
        on_device,
        mesh=mesh,
        in_specs=(
            P(("groups", "seq"), "fsdp"),
            P(("groups", "seq"), "fsdp"),
            P(("groups", "seq"), "fsdp"),
            P("fsdp", "seq"),
            P(("groups", "seq"), None),
        ),
        out_specs=(
            P(("groups", "seq"), None),
            P(("groups", "seq"), "fsdp"),
            P(("groups", "seq"), "fsdp"),
            P(("groups", "seq"), "fsdp"),
            P(("groups", "fsdp"), "seq"),
        ),
        check_vma=False,
    )
```

profile of v0, /device:TPU:0, one launch (start us, length us, event | category | flops | bytes accessed | tf_op | source)
XLA Modules:
  0.0 263.5 jit_solution(11399038725965434711)
XLA Ops:
  7.2 0.0 copy-start
  7.2 0.0 copy-start.2
  7.2 0.0 all-gather.6.cloned.1.call-start
  7.2 0.7 all-gather.6.cloned.1.call-update
  7.9 0.0 all-gather.8.cloned.1.call-start
  8.0 1.1 copy.60
  9.1 0.3 copy.35
  9.4 0.0 copy-done.2
  9.5 0.0 copy-start.3
  9.5 1.0 convolution_convert_fusion.3
  10.5 0.0 all-gather.8.cloned.1.call-update
  10.5 0.0 copy-start.1
  10.5 0.0 all-gather.10.cloned.1.call-start
  10.6 49.6 %all-gather.6.cloned.1.call-done = bf16[1024,2048]{1,0:T(8,128)(2,1)} async-done(((bf16[1024,256]{1,0:T(8,128)(2,1)}), bf16[1024,2048]{1,0:T(8,128)(2,1)}) %all-gather.6.cloned.1.call-update) | async-done | bytes 4194320 | tf_op jit(solution)/shard_map/all_gather | solution.py:42
  60.2 0.0 copy-done
  60.2 4.3 %convolution_convert_fusion.1 = bf16[256,1024]{1,0:T(8,128)(2,1)} fusion(bf16[256,2048]{1,0:T(8,128)(2,1)S(1)} %copy-done, bf16[1024,2048]{1,0:T(8,128)(2,1)} %all-gather.6.cloned.1.call-done), kind=kOutput, calls=%fused_computation.24 | convolution fusion | flops 1074003968 | bytes 5767168 | tf_op jit(solution)/shard_map/dot_general | solution.py:43
  64.4 0.0 copy-done.3
  64.4 1.2 copy.56
  65.7 0.0 copy-start.10
  65.7 0.0 copy-done.1
  65.7 0.3 fusion.11
  66.0 0.8 copy.46
  66.8 0.0 all-gather.10.cloned.1.call-update
  66.9 0.0 all-reduce.2.cloned.1.call-start
  66.9 0.0 copy-done.10
  67.0 0.5 select_convert_fusion.1
  67.4 0.0 copy-start.5
  67.4 1.0 copy-done.5
  68.4 1.5 convolution_bitcast_fusion.2
  69.9 19.8 %all-gather.8.cloned.1.call-done = bf16[64,128,128]{2,1,0:T(8,128)(2,1)} async-done(((bf16[8,128,128]{2,1,0:T(8,128)(2,1)}), bf16[64,128,128]{2,1,0:T(8,128)(2,1)}) %all-gather.8.cloned.1.call-update) | async-done | bytes 2097168 | tf_op jit(solution)/shard_map/all_gather | solution.py:18
  89.7 1.9 fusion.7
  91.6 0.0 copy-start.9
  91.6 0.8 copy-done.9
  92.4 4.4 %convolution_convert_fusion = bf16[256,2048]{1,0:T(8,128)(2,1)} fusion(bf16[256,1024]{0,1:T(8,128)(2,1)S(1)} %bitcast.130, bf16[1024,2048]{1,0:T(8,128)(2,1)} %all-gather.6.cloned.1.call-done), kind=kOutput, calls=%fused_computation.3 | convolution fusion | flops 1074266112 | bytes 5767168 | tf_op jit(solution)/shard_map/dot_general | solution.py:63
  96.8 0.0 all-reduce.2.cloned.1.call-update
  96.9 0.0 reduce-scatter.2.cloned.1.call-start
  96.9 5.6 %multiply_bitcast_fusion = f32[2048,1024]{0,1:T(8,128)} fusion(bf16[256,1024]{0,1:T(8,128)(2,1)} %bitcast.131, bf16[256,2048]{1,0:T(8,128)(2,1)S(1)} %copy-done), kind=kOutput, calls=%fused_computation.2 | convolution fusion | flops 1075838976 | bytes 9961472 | tf_op jit(solution)/shard_map/dot_general | solution.py:66
  102.5 0.0 reduce-scatter.2.cloned.1.call-update
  102.5 0.0 copy-start.4
  102.5 0.5 select_convert_fusion
  103.0 0.5 copy-done.4
  103.6 0.5 convolution_bitcast_fusion.1
  104.0 1.4 fusion.8
  105.4 2.1 copy.51
  107.5 2.7 %convolution_bitcast_fusion = f32[256,8,128]{0,2,1:T(8,128)} fusion(bf16[8,256,256]{2,1,0:T(8,128)(2,1)} %copy-done.8, bf16[256,1024]{1,0:T(8,128)(2,1)S(1)} %copy-done.1), kind=kOutput, calls=%fused_computation.17 | convolution fusion | flops 134217728 | bytes 2621440 | tf_op jit(solution)/shard_map/hts,thd->shd/dot_general | solution.py:81
  110.2 0.0 copy-done.6
  110.2 1.4 fusion.32
  111.5 8.4 %all-gather.10.cloned.1.call-done = bf16[64,128,128]{2,1,0:T(8,128)(2,1)} async-done(((bf16[8,128,128]{2,1,0:T(8,128)(2,1)}), bf16[64,128,128]{2,1,0:T(8,128)(2,1)}) %all-gather.10.cloned.1.call-update) | async-done | bytes 2097168 | tf_op jit(solution)/shard_map/all_gather | solution.py:18
  120.0 7.7 %while.23 = (s32[]{:T(128)}, f32[8,128,128]{2,1,0:T(8,128)S(1)}, s32[]{:T(128)}, bf16[8,8,128,128]{3,2,1,0:T(8,128)(2,1)}, s32[]{:T(128)}, /*index=5*/s32[]{:T(128)}, s32[]{:T(128)}, s32[]{:T(128)}) while((s32[]{:T(128)}, f32[8,128,128]{2,1,0:T(8,128)S(1)}, s32[]{:T(128)}, bf16[8,8,128,128]{3,2,1,0:T(8,128)(2,1)}, s32[]{:T(128)}, ...), condition=%wide.region_4.5_spmd, body=%wide.region_3.4_spmd.sunk | while | flops 262150 | bytes 1310863 | solution.py:25
  120.0 1.1 convert_add_fusion.5
  121.1 1.1 convert_add_fusion.5
  122.2 1.1 convert_add_fusion.5
  123.3 1.1 convert_add_fusion.5
  124.4 1.1 convert_add_fusion.5
  125.4 1.1 convert_add_fusion.5
  126.5 1.1 convert_add_fusion.5
  127.6 2.7 %fusion.9 = bf16[256,8,128]{0,2,1:T(8,128)(2,1)} fusion(f32[256,8,128]{0,2,1:T(8,128)} %convolution_bitcast_fusion, f32[8,128,128]{2,1,0:T(8,128)S(1)} %get-tuple-element.85, bf16[256,1024]{1,0:T(8,128)(2,1)S(1)} %copy-done.2), kind=kOutput, calls=%fused_computation.22 | convolution fusion | flops 403439616 | bytes 2621440 | tf_op jit(solution)/shard_map/the,hde->thd/dot_general | solution.py:83
  130.4 2.0 copy.52
  132.4 0.0 copy-done.7
  132.4 1.7 fusion.10
  134.1 1.0 copy.53
  135.1 27.1 %all-reduce.2.cloned.1.call-done = bf16[256,2048]{1,0:T(8,128)(2,1)} async-done(((bf16[256,2048]{1,0:T(8,128)(2,1)}), bf16[256,2048]{1,0:T(8,128)(2,1)}) %all-reduce.2.cloned.1.call-update) | async-done | bytes 1048592 | tf_op jit(solution)/shard_map/psum | solution.py:64
  162.2 92.5 %reduce-scatter.2.cloned.1.call-done = f32[256,1024]{0,1:T(8,128)} async-done(((f32[2048,1024]{0,1:T(8,128)}), f32[256,1024]{0,1:T(8,128)}) %reduce-scatter.2.cloned.1.call-update) | async-done | bytes 1048592 | tf_op jit(solution)/shard_map/reduce_scatter | solution.py:65
  254.7 2.3 copy.114
  (8 shorter events, 0.1 us)
Async XLA Ops:
  7.2 53.0 %copy-start = (bf16[256,2048]{1,0:T(8,128)(2,1)S(1)}, bf16[256,2048]{1,0:T(8,128)(2,1)}, u32[]{:S(2)}) copy-start(bf16[256,2048]{1,0:T(8,128)(2,1)} %param.13) | copy-start | bytes 3145732
  7.2 2.3 copy-start.2
  7.2 53.0 %all-gather.6.cloned.1.call-start = ((), (), s32[]{:S(2)}) async-start(), calls=%async_computation.1 | async-start | bytes 4718592 | tf_op jit(solution)/shard_map/all_gather | solution.py:42
  7.9 81.8 %all-gather.8.cloned.1.call-start = ((), (), s32[]{:S(2)}) async-start(), calls=%async_computation.4 | async-start | bytes 2359296 | tf_op jit(solution)/shard_map/all_gather | solution.py:18
  9.5 55.0 %copy-start.3 = (bf16[256,8,128]{0,2,1:T(8,128)(2,1)}, bf16[256,8,128]{0,2,1:T(8,128)(2,1)S(1)}, u32[]{:S(2)}) copy-start(bf16[256,8,128]{0,2,1:T(8,128)(2,1)S(1)} %copy.35) | copy-start | bytes 1572868
  10.5 55.2 %copy-start.1 = (bf16[256,1024]{1,0:T(8,128)(2,1)S(1)}, bf16[256,1024]{1,0:T(8,128)(2,1)}, u32[]{:S(2)}) copy-start(bf16[256,1024]{1,0:T(8,128)(2,1)} %param.9) | copy-start | bytes 1572868
  10.5 109.4 %all-gather.10.cloned.1.call-start = ((), (), s32[]{:S(2)}) async-start(), calls=%async_computation.5 | async-start | bytes 2359296 | tf_op jit(solution)/shard_map/all_gather | solution.py:18
  65.7 1.3 copy-start.10
  66.9 95.4 %all-reduce.2.cloned.1.call-start = ((), (), s32[]{:S(2)}) async-start(), calls=%async_computation.2 | async-start | bytes 2097152 | tf_op jit(solution)/shard_map/psum | solution.py:64
  67.4 1.0 copy-start.5
  91.6 0.8 copy-start.9
  96.9 157.8 %reduce-scatter.2.cloned.1.call-start = ((), (), s32[]{:S(2)}) async-start(), calls=%async_computation.3 | async-start | bytes 9437184 | tf_op jit(solution)/shard_map/reduce_scatter | solution.py:65
  102.5 1.0 copy-start.4
  103.6 1.9 copy-start.8
  107.5 2.7 %copy-start.6 = (bf16[8,256,256]{2,1,0:T(8,128)(2,1)S(1)}, bf16[8,256,256]{2,1,0:T(8,128)(2,1)}, u32[]{:S(2)}) copy-start(bf16[8,256,256]{2,1,0:T(8,128)(2,1)} %copy-done.5) | copy-start | bytes 3145732
  127.6 4.8 %copy-start.7 = (f32[8,128,256]{2,1,0:T(8,128)S(1)}, f32[8,128,256]{2,1,0:T(8,128)}, u32[]{:S(2)}) copy-start(f32[8,128,256]{2,1,0:T(8,128)} %fusion.32) | copy-start | bytes 3145732
Sparse Core Ops, SparseCore 0:
  9.6 50.4 all-gather.5
  62.3 27.3 all-gather.7
  91.3 28.5 all-gather.9
  122.6 39.5 all-reduce.1
  165.0 89.6 reduce-scatter.1
where the time goes:
time: 264 us
  waiting for transfers between devices  198 us (75%)
  matrix products  30.1 us (11%)
  between operations  14 us (5%)
  local copies, waits for them, and re-layouts  13.4 us (5%)
  other arithmetic  7.53 us (3%)
    reduce_scatter x1, waiting for transfers between devices, on_device(): lax.psum_scatter(lax.dot_general(out_grad, attention, (((0,), (0,)), ((),...  92.5 us
    all_gather x1, waiting for transfers between devices, on_device(): full_weight = lax.all_gather(out_weight, 'seq', axis=1, tiled=True)  49.6 us
    all_gather x2, waiting for transfers between devices, prefix_2(): gathered = lax.all_gather(value.astype(jnp.bfloat16), axis)  28.2 us
    psum x1, waiting for transfers between devices, on_device(): mixed = lax.psum(partial_out.astype(jnp.bfloat16), 'fsdp')  27.1 us
    unnamed x27, local copies, waits for them, and re-layouts  10.9 us
    add x7, other arithmetic, added(): return jax.tree.map(lambda first, second: first + second, earlier, later)  7.5 us
    dot_general x1, matrix products, on_device(): lax.dot_general(out_grad, attention, (((0,), (0,)), ((), ())), preferred_...  5.57 us
  transfers between devices with their start and end apart: 5, of which 5 were waited for; matrix products, arithmetic and copies ran while one was open for 18% of the time, Pallas kernels for 0%

commit v1 on v0

--- a/solution.py
+++ b/solution.py
@@ -1,14 +1,378 @@
+import functools
 import math
 
 import jax
 import jax.numpy as jnp
 from jax import lax
+from jax.experimental import pallas as pl
+from jax.experimental.pallas import tpu as pltpu
 from jax.sharding import PartitionSpec as P
 
 HD = 128
 
 
 HIGH = lax.Precision.HIGHEST
+
+
+MESH = pl.DeviceIdType.MESH
+BF = jnp.bfloat16
+F32 = jnp.float32
+CHUNKS = 4
+
+
+def mm(a, b, dims):
+    return lax.dot_general(a, b, ((dims[0], dims[1]), ((), ())), preferred_element_type=F32)
+
+
+NN = ((1,), (0,))
+NT = ((1,), (1,))
+TN = ((0,), (0,))
+
+
+def message_ids(nz):
+    ids = {}
+
+    def add(*name):
+        ids[name] = len(ids)
+
+    for d in range(1, nz):
+        for way in ("up", "dn"):
+            for kind in ("z", "y", "s", "ys"):
+                add("w", kind, way, d)
+    add("w", "own")
+    for t in range(nz):
+        add("og", t)
+    for name in ("S", "T", "att", "pre", "pres", "suf", "sufs"):
+        add(name)
+    for t in range(nz):
+        for r in range(CHUNKS):
+            add("r", "up", t, r)
+            add("r", "dn", t, r)
+    for j in range(2 * nz):
+        add("mix", j)
+    return ids
+
+
+def kernel(
+    nz, ids, factor, grad_factor,
+    q, k, v, w, og,
+    mixed, qg, kg, vg, wg,
+    wf, og_chip, att, s_own, s_sib, t_own, t_sib,
+    pre_in, pre_sib, pre_out, suf_in, suf_sib, suf_out,
+    prefix, sc, grads, acc, kg32, vg32, m, up_in, up_out, dn_in, dn_out, mix_out, mix_in,
+    send, recv,
+):
+    length, width = q.shape
+    heads = width // HD
+    half = heads // 2
+    hrows = width // 2
+    cols = w.shape[1]
+    rows = width // CHUNKS
+    g = lax.axis_index("groups")
+    s = lax.axis_index("seq")
+    f = lax.axis_index("fsdp")
+    z = lax.div(s, 2)
+    c = lax.rem(s, 2)
+    o = 1 - c
+    sib = {"seq": z * 2 + o}
+    upper = {"seq": s + 2}
+    lower = {"seq": s - 2}
+    ypart = {"groups": 1 - g}
+    xpart = {"fsdp": 1 - f}
+    last = nz - 1
+
+    def make(name, src, dst, to):
+        i = ids[name]
+        return pltpu.make_async_remote_copy(
+            src_ref=src, dst_ref=dst, send_sem=send.at[i], recv_sem=recv.at[i],
+            device_id=to, device_id_type=MESH,
+        )
+
+    started = []
+
+    def go(name, src, dst, to, cond=None):
+        started.append((name, src, dst, to, cond))
+        if cond is None:
+            make(name, src, dst, to).start()
+        else:
+            @pl.when(cond)
+            def _():
+                make(name, src, dst, to).start()
+
+    def got(name, dst, to, src=None):
+        make(name, dst if src is None else src, dst, to).wait_recv()
+
+    def hs(h):
+        return slice(h * HD, (h + 1) * HD)
+
+    for h in range(heads):
+        s_own[h] = mm(k[:, hs(h)], v[:, hs(h)], TN).astype(BF)
+
+    barrier = pltpu.get_barrier_semaphore()
+    for to in (sib, ypart, xpart):
+        pl.semaphore_signal(barrier, inc=1, device_id=to, device_id_type=MESH)
+
+    @pl.when(z > 0)
+    def _():
+        pl.semaphore_signal(barrier, inc=1, device_id=lower, device_id_type=MESH)
+
+    @pl.when(z < last)
+    def _():
+        pl.semaphore_signal(barrier, inc=1, device_id=upper, device_id_type=MESH)
+
+    pl.semaphore_wait(barrier, 3 + (z > 0).astype(jnp.int32) + (z < last).astype(jnp.int32))
+
+    def wslot(chip, core, h):
+        return wf.at[chip * 2 + core, pl.ds(pl.multiple_of(h * hrows, hrows), hrows)]
+
+    go(("S",), s_own, s_sib, sib)
+    mine = w.at[pl.ds(pl.multiple_of(g * hrows, hrows), hrows)]
+    go(("w", "z", "up", 1), mine, wslot(z, c, g), upper, z < last)
+    go(("w", "z", "dn", 1), mine, wslot(z, c, g), lower, z > 0)
+    go(("w", "own"), w, wf.at[s], sib)
+    for t in range(nz):
+        theirs = pl.ds(pl.multiple_of((2 * t + o) * cols, cols), cols)
+        go(
+            ("og", t), og.at[:, theirs],
+            og_chip.at[pl.ds(pl.multiple_of(c * length, length), length), t * cols:(t + 1) * cols],
+            sib,
+        )
+    wf[s] = w[...]
+    own_rows = pl.ds(pl.multiple_of(c * length, length), length)
+    for t in range(nz):
+        own = pl.ds(pl.multiple_of((2 * t + c) * cols, cols), cols)
+        og_chip[own_rows, t * cols:(t + 1) * cols] = og[:, own]
+
+    lo = pl.multiple_of(c * half, half)
+    mine_h = pl.ds(lo, half)
+
+    def chain(name, out, own, other, buf_in, buf_sib, ok_in, ok_out, to):
+        @pl.when(ok_in)
+        def _():
+            got((name,), buf_in, sib)
+            out[...] = (
+                buf_in[...].astype(F32) + own[mine_h].astype(F32) + other[mine_h].astype(F32)
+            ).astype(BF)
+
+        @pl.when(jnp.logical_not(ok_in))
+        def _():
+            out[...] = (own[mine_h].astype(F32) + other[mine_h].astype(F32)).astype(BF)
+
+        go((name,), out, buf_in, to, ok_out)
+        go((name + "s",), buf_in, buf_sib, sib, ok_in)
+
+    def w_step(d):
+        for way, ok, more, chip, to in (
+            ("up", z >= d, z < last, z - d, upper),
+            ("dn", z + d <= last, z > 0, z + d, lower),
+        ):
+            place = wslot(chip, c, g)
+
+            @pl.when(ok)
+            def _():
+                got(("w", "z", way, d), place, sib)
+            if d < last:
+                go(("w", "z", way, d + 1), place, place, to, jnp.logical_and(ok, more))
+            go(("w", "y", way, d), place, place, ypart, ok)
+            go(("w", "s", way, d), place, place, sib, ok)
+
+    def w_y(d):
+        for way, ok, chip in (("up", z >= d, z - d), ("dn", z + d <= last, z + d)):
+            place = wslot(chip, c, 1 - g)
+
+            @pl.when(ok)
+            def _():
+                got(("w", "y", way, d), place, sib)
+            go(("w", "ys", way, d), place, place, sib, ok)
+
+    def w_sib():
+        got(("w", "own"), wf.at[z * 2 + o], sib)
+        for d in range(1, nz):
+            for way, ok, chip in (("up", z >= d, z - d), ("dn", z + d <= last, z + d)):
+                @pl.when(ok)
+                def _():
+                    got(("w", "s", way, d), wslot(chip, o, g), sib)
+                    got(("w", "ys", way, d), wslot(chip, o, 1 - g), sib)
+
+    got(("S",), s_sib, sib)
+    chain("pre", pre_out, s_own, s_sib, pre_in, pre_sib, z > 0, z < last, upper)
+    w_step(1)
+
+    def joined(buf_in, buf_sib, other, ok, name, with_sib, out):
+        @pl.when(ok)
+        def _():
+            got((name + "s",), buf_sib, sib)
+            add = jnp.where(with_sib, 1.0, 0.0).astype(F32)
+            out[mine_h] = (buf_in[...].astype(F32) + add * other[mine_h].astype(F32)).astype(BF)
+            theirs_h = pl.ds(pl.multiple_of(o * half, half), half)
+            out[theirs_h] = (buf_sib[...].astype(F32) + add * other[theirs_h].astype(F32)).astype(BF)
+
+        @pl.when(jnp.logical_not(ok))
+        def _():
+            add = jnp.where(with_sib, 1.0, 0.0).astype(F32)
+            out[...] = (add * other[...].astype(F32)).astype(BF)
+
+    joined(pre_in, pre_sib, s_sib, z > 0, "pre", c == 1, prefix)
+    causal = lax.broadcasted_iota(jnp.int32, (length, length), 0) >= lax.broadcasted_iota(
+        jnp.int32, (length, length), 1
+    )
+
+    for h in range(heads):
+        qh, kh, vh = q[:, hs(h)], k[:, hs(h)], v[:, hs(h)]
+        scores = jnp.where(causal, mm(qh, kh, NT) * factor, 0.0).astype(BF)
+        sc[h] = scores
+        out = mm(scores, vh, NN) + mm(qh, prefix[h], NN) * factor
+        att[own_rows, hs(h)] = out.astype(BF)
+    go(("att",), att.at[own_rows], att.at[own_rows], sib)
+    w_y(1)
+    w_step(2) if nz > 2 else None
+
+    sib_rows = pl.ds(pl.multiple_of(o * length, length), length)
+    got(("att",), att.at[sib_rows], sib)
+    for t in range(nz):
+        got(("og", t), og_chip.at[sib_rows, t * cols:(t + 1) * cols], sib)
+    for r in range(CHUNKS):
+        m[r * rows:(r + 1) * rows] = (
+            mm(att[:, r * rows:(r + 1) * rows], og_chip[...], TN) * grad_factor
+        )
+
+    def rs(way, t, r, origin):
+        rr = slice(r * rows, (r + 1) * rows)
+        buf_in, buf_out = (up_in, up_out) if way == "up" else (dn_in, dn_out)
+        to = upper if way == "up" else lower
+        first = z == 0 if way == "up" else z == last
+        ahead = z < t if way == "up" else z > t
+        tc = slice(t * cols, (t + 1) * cols)
+        name = ("r", way, t, r)
+        if origin:
+            ok = jnp.logical_and(first, ahead)
+
+            @pl.when(ok)
+            def _():
+                buf_out[t, rr] = m[rr, tc].astype(BF)
+        else:
+            ok = jnp.logical_and(jnp.logical_not(first), ahead)
+
+            @pl.when(ok)
+            def _():
+                got(name, buf_in.at[t, rr], sib)
+                buf_out[t, rr] = (m[rr, tc] + buf_in[t, rr].astype(F32)).astype(BF)
+        go(name, buf_out.at[t, rr], buf_in.at[t, rr], to, ok)
+
+    def rs_round(i, origin):
+        for r in range(CHUNKS):
+            rs("up", last - i, r, origin)
+            rs("dn", i, r, origin)
+
+    for i in range(nz - 1):
+        rs_round(i, True)
+    for d in range(2, nz):
+        w_y(d)
+        if d + 1 < nz:
+            w_step(d + 1)
+    w_sib()
+
+    for j in range(2 * nz):
+        part = mm(og[:, j * cols:(j + 1) * cols], wf[j], NT)
+        if j == 0:
+            acc[...] = part
+        else:
+            acc[...] += part
+    grads[...] = acc[...].astype(BF)
+    for h in range(heads):
+        t_own[h] = mm(q[:, hs(h)], grads[:, hs(h)], TN).astype(BF)
+    go(("T",), t_own, t_sib, sib)
+    for j in range(2 * nz):
+        mix_out[j] = mm(att[own_rows, :], wf[j], NN).astype(BF)
+        go(("mix", j), mix_out.at[j], mix_in.at[j], xpart)
+    got(("T",), t_sib, sib)
+    rs_round(0, False)
+    chain("suf", suf_out, t_own, t_sib, suf_in, suf_sib, z < last, z > 0, lower)
+
+    for h in range(heads):
+        qh, kh, vh, gh = q[:, hs(h)], k[:, hs(h)], v[:, hs(h)], grads[:, hs(h)]
+        mixing = jnp.where(causal, mm(gh, vh, NT) * factor, 0.0).astype(BF)
+        qg[:, hs(h)] = (mm(mixing, kh, NN) + mm(gh, prefix[h], NT) * factor).astype(BF)
+        kg32[:, hs(h)] = mm(mixing, qh, TN)
+        vg32[:, hs(h)] = mm(sc[h], gh, TN)
+
+    for i in range(1, nz - 1):
+        rs_round(i, False)
+
+    joined(suf_in, suf_sib, t_sib, z < last, "suf", c == 0, prefix)
+    for h in range(heads):
+        kh, vh = k[:, hs(h)], v[:, hs(h)]
+        kg[:, hs(h)] = (kg32[:, hs(h)] + mm(vh, prefix[h], NT) * factor).astype(BF)
+        vg[:, hs(h)] = (vg32[:, hs(h)] + mm(kh, prefix[h], NN) * factor).astype(BF)
+
+    for j in range(2 * nz):
+        got(("mix", j), mix_in.at[j], xpart)
+        mixed[:, j * cols:(j + 1) * cols] = (
+            mix_out[j].astype(F32) + mix_in[j].astype(F32)
+        ).astype(BF)
+
+    here = pl.ds(pl.multiple_of(z * cols, cols), cols)
+    for r in range(CHUNKS):
+        rr = slice(r * rows, (r + 1) * rows)
+        wg[rr] = m[rr, here]
+        for way, ok, buf in (("up", z > 0, up_in), ("dn", z < last, dn_in)):
+            for t in range(nz):
+                @pl.when(jnp.logical_and(ok, z == t))
+                def _():
+                    got(("r", way, t, r), buf.at[t, rr], sib)
+                    wg[rr] += buf[t, rr].astype(F32)
+
+    for name, src, dst, to, cond in started:
+        if cond is None:
+            make(name, src, dst, to).wait_send()
+        else:
+            @pl.when(cond)
+            def _():
+                make(name, src, dst, to).wait_send()
+
+
+def fused(query_rows, key_rows, value_rows, out_weight, out_grad):
+    length, width = query_rows.shape
+    model = out_grad.shape[1]
+    cols = out_weight.shape[1]
+    nseq = lax.axis_size("seq")
+    nz = nseq // 2
+    total = length * nseq
+    heads = width // HD
+    half = heads // 2
+    ids = message_ids(nz)
+    state = (heads, HD, HD)
+    hstate = (half, HD, HD)
+    vm = pltpu.VMEM
+    scratch = [
+        vm((nseq, width, cols), BF), vm((2 * length, nz * cols), BF), vm((2 * length, width), BF),
+        vm(state, BF), vm(state, BF), vm(state, BF), vm(state, BF),
+        vm(hstate, BF), vm(hstate, BF), vm(hstate, BF), vm(hstate, BF), vm(hstate, BF), vm(hstate, BF),
+        vm(state, BF), vm((heads, length, length), BF), vm((length, width), BF),
+        vm((length, width), F32), vm((length, width), F32), vm((length, width), F32),
+        vm((width, nz * cols), F32),
+        vm((nz, width, cols), BF), vm((nz, width, cols), BF),
+        vm((nz, width, cols), BF), vm((nz, width, cols), BF),
+        vm((nseq, length, cols), BF), vm((nseq, length, cols), BF),
+        pltpu.SemaphoreType.DMA((len(ids),)), pltpu.SemaphoreType.DMA((len(ids),)),
+    ]
+    block = jax.ShapeDtypeStruct((length, width), BF)
+    spec = pl.BlockSpec(memory_space=pltpu.VMEM)
+    return pl.pallas_call(
+        functools.partial(
+            kernel, nz, ids, 1.0 / math.sqrt(HD * total), 1.0 / math.sqrt(total)
+        ),
+        out_shape=(
+            jax.ShapeDtypeStruct((length, model), BF), block, block, block,
+            jax.ShapeDtypeStruct((width, cols), F32),
+        ),
+        in_specs=[spec] * 5,
+        out_specs=(spec,) * 5,
+        scratch_shapes=scratch,
+        compiler_params=pltpu.CompilerParams(
+            collective_id=0, has_side_effects=True, vmem_limit_bytes=52 * 2**20
+        ),
+    )(query_rows, key_rows, value_rows, out_weight, out_grad)
 
 
 def prefix_2(value, axis, join, neutral, backward):
@@ -90,9 +454,17 @@
     return (mixed, query_grad, key_grad, value_grad, weight_grad)
 
 
+def fits(mesh):
+    shape = mesh.shape
+    return (
+        shape["groups"] == 2 and shape["fsdp"] == 2 and shape["seq"] % 2 == 0
+        and 2 < shape["seq"] <= 8
+    )
+
+
 def solution(mesh):
     return jax.shard_map(
-        on_device,
+        fused if fits(mesh) else on_device,
         mesh=mesh,
         in_specs=(
             P(("groups", "seq"), "fsdp"),

time: 264 us -> 96.5 us (0.37)
  waiting for transfers between devices: 198 us -> 0 us
  Pallas kernels: 0 us -> 88.5 us
  matrix products: 30.1 us -> 0 us
  between operations: 14 us -> 0.64 us
  local copies, waits for them, and re-layouts: 13.4 us -> 5.66 us
  other arithmetic: 7.53 us -> 0 us
    reduce_scatter x1 -> x0, waiting for transfers between devices: 92.5 us -> none  [on_device(): lax.psum_scatter(lax.dot_general(out_grad, attention, (((0,), (0,)), ((),...]
    pallas_call x0 -> x1, Pallas kernels: none -> 88.5 us  [fused(): pl.pallas_call(functools.partial(kernel, nz, ids, 1.0 / math.sqrt(HD * to...]
    all_gather x3 -> x0, waiting for transfers between devices: 77.8 us -> none  [the longest x1 49.6 us: on_device(): full_weight = lax.all_gather(out_weight, 'seq', axis=1, tiled=True)]
    dot_general x15 -> x0, matrix products: 30.1 us -> none  [the longest x1 5.57 us: on_device(): lax.dot_general(out_grad, attention, (((0,), (0,)), ((), ())), preferred_...]
    psum x1 -> x0, waiting for transfers between devices: 27.1 us -> none  [on_device(): mixed = lax.psum(partial_out.astype(jnp.bfloat16), 'fsdp')]
    add x7 -> x0, other arithmetic: 7.5 us -> none  [added(): return jax.tree.map(lambda first, second: first + second, earlier, later)]
    unnamed x27 -> x7, local copies, waits for them, and re-layouts: 10.9 us -> 5.66 us
  transfers between devices with their start and end apart: 5 -> 0, of which waited for: 5 -> 0; matrix products, arithmetic and copies ran while one was open for 18% -> 0% of each run, Pallas kernels for 0% -> 0%
where the time goes in v1:
time: 96.5 us; the launch traced here: 94.8 us
  Pallas kernels  88.5 us (92%)
  local copies, waits for them, and re-layouts  5.66 us (6%)
    pallas_call x1, Pallas kernels, fused(): pl.pallas_call(functools.partial(kernel, nz, ids, 1.0 / math.sqrt(HD * to...  88.5 us
    unnamed x7, local copies, waits for them, and re-layouts  5.66 us

profile of v1, /device:TPU:0, one launch (start us, length us, event | category | flops | bytes accessed | tf_op | source)
XLA Modules:
  0.0 94.8 jit_solution(12157683688762042812)
XLA Ops:
  0.6 88.5 %shard_map.92 = (bf16[256,2048]{1,0:T(8,128)(2,1)}, bf16[256,1024]{1,0:T(8,128)(2,1)S(1)}, bf16[256,1024]{1,0:T(8,128)(2,1)S(1)}, bf16[256,1024]{1,0:T(8,128)(2,1)S(1)}, f32[1024,256]{1,0:T(8,128)}) custom-call(bf16[256,1024]{1,0:T(8,128)(2,1)} %q.1, bf16[256,1024]{1,0:T(8,128)(2,1)} %k.1, bf16[256,1024]{1,0:T(8,128)(2,1)} %v.1, bf16[1024,256]{1,0:T(8,128)(2,1)} %w.1, ...), custom_call_target="tpu_custom_call" | custom-call | tf_op jit(solution)/shard_map/pallas_call | solution.py:361
  89.2 2.3 %copy.15 = bf16[256,2048]{1,0:T(8,128)(2,1)} copy(bf16[256,2048]{1,0:T(8,128)(2,1)} %get-tuple-element.10) | data formatting | bytes 2097152
  91.5 0.8 copy.16
  92.3 0.0 copy-start
  92.3 0.8 copy.17
  93.0 0.8 copy.18
  93.8 0.0 copy-done
  93.8 1.0 %copy.19 = f32[1024,256]{1,0:T(8,128)} copy(f32[1024,256]{1,0:T(8,128)S(1)} %copy-done) | data formatting | bytes 2097152
Async XLA Ops:
  92.3 1.6 %copy-start = (f32[1024,256]{1,0:T(8,128)S(1)}, f32[1024,256]{1,0:T(8,128)}, u32[]{:S(2)}) copy-start(f32[1024,256]{1,0:T(8,128)} %get-tuple-element.14) | copy-start | bytes 3145732

commit v2 on v1

--- a/solution.py
+++ b/solution.py
@@ -29,7 +29,7 @@
 TN = ((0,), (0,))
 
 
-def message_ids(nz):
+def message_ids(nz, half):
     ids = {}
 
     def add(*name):
@@ -42,14 +42,19 @@
     add("w", "own")
     for t in range(nz):
         add("og", t)
-    for name in ("S", "T", "att", "pre", "pres", "suf", "sufs"):
+    for name in ("S", "T", "att"):
         add(name)
+    for name in ("pre", "pres", "suf", "sufs"):
+        for h in range(half):
+            add(name, h)
     for t in range(nz):
         for r in range(CHUNKS):
             add("r", "up", t, r)
             add("r", "dn", t, r)
-    for j in range(2 * nz):
-        add("mix", j)
+    for d in range(nz):
+        for way in ("up", "dn"):
+            for core in (0, 1):
+                add("mix", way, d, core)
     return ids
 
 
@@ -146,20 +151,26 @@
     lo = pl.multiple_of(c * half, half)
     mine_h = pl.ds(lo, half)
 
-    def chain(name, out, own, other, buf_in, buf_sib, ok_in, ok_out, to):
-        @pl.when(ok_in)
-        def _():
-            got((name,), buf_in, sib)
-            out[...] = (
-                buf_in[...].astype(F32) + own[mine_h].astype(F32) + other[mine_h].astype(F32)
-            ).astype(BF)
-
-        @pl.when(jnp.logical_not(ok_in))
+    def origin(name, out, own, other, buf_in, ok_in, to):
+        first = jnp.logical_not(ok_in)
+
+        @pl.when(first)
         def _():
             out[...] = (own[mine_h].astype(F32) + other[mine_h].astype(F32)).astype(BF)
 
-        go((name,), out, buf_in, to, ok_out)
-        go((name + "s",), buf_in, buf_sib, sib, ok_in)
+        for h in range(half):
+            go((name, h), out.at[h], buf_in.at[h], to, first)
+
+    def relay(name, out, own, other, buf_in, buf_sib, ok_in, ok_out, to):
+        for h in range(half):
+            @pl.when(ok_in)
+            def _():
+                got((name, h), buf_in.at[h], sib)
+                out[h] = (
+                    buf_in[h].astype(F32) + own[lo + h].astype(F32) + other[lo + h].astype(F32)
+                ).astype(BF)
+            go((name, h), out.at[h], buf_in.at[h], to, jnp.logical_and(ok_in, ok_out))
+            go((name + "s", h), buf_in.at[h], buf_sib.at[h], sib, ok_in)
 
     def w_step(d):
         for way, ok, more, chip, to in (
@@ -185,23 +196,34 @@
                 got(("w", "y", way, d), place, sib)
             go(("w", "ys", way, d), place, place, sib, ok)
 
-    def w_sib():
-        got(("w", "own"), wf.at[z * 2 + o], sib)
-        for d in range(1, nz):
-            for way, ok, chip in (("up", z >= d, z - d), ("dn", z + d <= last, z + d)):
-                @pl.when(ok)
-                def _():
-                    got(("w", "s", way, d), wslot(chip, o, g), sib)
-                    got(("w", "ys", way, d), wslot(chip, o, 1 - g), sib)
-
-    got(("S",), s_sib, sib)
-    chain("pre", pre_out, s_own, s_sib, pre_in, pre_sib, z > 0, z < last, upper)
-    w_step(1)
+    def shard(way, d, core, j, ok):
+        jc = pl.ds(pl.multiple_of(j * cols, cols), cols)
+
+        @pl.when(ok)
+        def _():
+            acc[...] += mm(og[:, jc], wf[j], NT)
+            mix_out[j] = mm(att[own_rows, :], wf[j], NN).astype(BF)
+        go(("mix", way, d, core), mix_out.at[j], mix_in.at[j], xpart, ok)
+
+    def shards(d):
+        for way, ok, chip in (("up", z >= d, z - d), ("dn", z + d <= last, z + d)):
+            shard(way, d, 0, chip * 2 + c, ok)
+
+            @pl.when(ok)
+            def _():
+                got(("w", "s", way, d), wslot(chip, o, g), sib)
+                got(("w", "ys", way, d), wslot(chip, o, 1 - g), sib)
+            shard(way, d, 1, chip * 2 + o, ok)
+
+    causal = lax.broadcasted_iota(jnp.int32, (length, length), 0) >= lax.broadcasted_iota(
+        jnp.int32, (length, length), 1
+    )
 
     def joined(buf_in, buf_sib, other, ok, name, with_sib, out):
         @pl.when(ok)
         def _():
-            got((name + "s",), buf_sib, sib)
+            for h in range(half):
+                got((name + "s", h), buf_sib.at[h], sib)
             add = jnp.where(with_sib, 1.0, 0.0).astype(F32)
             out[mine_h] = (buf_in[...].astype(F32) + add * other[mine_h].astype(F32)).astype(BF)
             theirs_h = pl.ds(pl.multiple_of(o * half, half), half)
@@ -212,26 +234,7 @@
             add = jnp.where(with_sib, 1.0, 0.0).astype(F32)
             out[...] = (add * other[...].astype(F32)).astype(BF)
 
-    joined(pre_in, pre_sib, s_sib, z > 0, "pre", c == 1, prefix)
-    causal = lax.broadcasted_iota(jnp.int32, (length, length), 0) >= lax.broadcasted_iota(
-        jnp.int32, (length, length), 1
-    )
-
-    for h in range(heads):
-        qh, kh, vh = q[:, hs(h)], k[:, hs(h)], v[:, hs(h)]
-        scores = jnp.where(causal, mm(qh, kh, NT) * factor, 0.0).astype(BF)
-        sc[h] = scores
-        out = mm(scores, vh, NN) + mm(qh, prefix[h], NN) * factor
-        att[own_rows, hs(h)] = out.astype(BF)
-    go(("att",), att.at[own_rows], att.at[own_rows], sib)
-    w_y(1)
-    w_step(2) if nz > 2 else None
-
-    sib_rows = pl.ds(pl.multiple_of(o * length, length), length)
-    got(("att",), att.at[sib_rows], sib)
-    for t in range(nz):
-        got(("og", t), og_chip.at[sib_rows, t * cols:(t + 1) * cols], sib)
-    for r in range(CHUNKS):
+    def m_step(r):
         m[r * rows:(r + 1) * rows] = (
             mm(att[:, r * rows:(r + 1) * rows], og_chip[...], TN) * grad_factor
         )
@@ -259,45 +262,63 @@
                 buf_out[t, rr] = (m[rr, tc] + buf_in[t, rr].astype(F32)).astype(BF)
         go(name, buf_out.at[t, rr], buf_in.at[t, rr], to, ok)
 
-    def rs_round(i, origin):
-        for r in range(CHUNKS):
+    def rs_round(r, origin):
+        for i in range(nz - 1):
             rs("up", last - i, r, origin)
             rs("dn", i, r, origin)
 
-    for i in range(nz - 1):
-        rs_round(i, True)
-    for d in range(2, nz):
-        w_y(d)
-        if d + 1 < nz:
-            w_step(d + 1)
-    w_sib()
-
-    for j in range(2 * nz):
-        part = mm(og[:, j * cols:(j + 1) * cols], wf[j], NT)
-        if j == 0:
-            acc[...] = part
-        else:
-            acc[...] += part
-    grads[...] = acc[...].astype(BF)
+    got(("S",), s_sib, sib)
+    origin("pre", pre_out, s_own, s_sib, pre_in, z > 0, upper)
     for h in range(heads):
+        scores = jnp.where(causal, mm(q[:, hs(h)], k[:, hs(h)], NT) * factor, 0.0).astype(BF)
+        sc[h] = scores
+        acc[:, hs(h)] = mm(scores, v[:, hs(h)], NN)
+    relay("pre", pre_out, s_own, s_sib, pre_in, pre_sib, z > 0, z < last, upper)
+    w_step(1)
+    joined(pre_in, pre_sib, s_sib, z > 0, "pre", c == 1, prefix)
+    for h in range(heads):
+        att[own_rows, hs(h)] = (acc[:, hs(h)] + mm(q[:, hs(h)], prefix[h], NN) * factor).astype(BF)
+    go(("att",), att.at[own_rows], att.at[own_rows], sib)
+    acc[...] = jnp.zeros_like(acc)
+    always = z >= 0
+    shard("up", 0, 0, s, always)
+    w_y(1)
+    sib_rows = pl.ds(pl.multiple_of(o * length, length), length)
+    got(("att",), att.at[sib_rows], sib)
+    for t in range(nz):
+        got(("og", t), og_chip.at[sib_rows, t * cols:(t + 1) * cols], sib)
+    m_step(0)
+    rs_round(0, True)
+    w_step(2)
+    for r in range(1, CHUNKS):
+        m_step(r)
+        rs_round(r, True)
+    got(("w", "own"), wf.at[z * 2 + o], sib)
+    shard("up", 0, 1, z * 2 + o, always)
+    shards(1)
+    w_y(2)
+    rs_round(0, False)
+    w_step(3)
+    shards(2)
+    w_y(3)
+    shards(3)
+
+    for h in range(heads):
+        grads[:, hs(h)] = acc[:, hs(h)].astype(BF)
         t_own[h] = mm(q[:, hs(h)], grads[:, hs(h)], TN).astype(BF)
     go(("T",), t_own, t_sib, sib)
-    for j in range(2 * nz):
-        mix_out[j] = mm(att[own_rows, :], wf[j], NN).astype(BF)
-        go(("mix", j), mix_out.at[j], mix_in.at[j], xpart)
+    rs_round(1, False)
     got(("T",), t_sib, sib)
-    rs_round(0, False)
-    chain("suf", suf_out, t_own, t_sib, suf_in, suf_sib, z < last, z > 0, lower)
-
+    origin("suf", suf_out, t_own, t_sib, suf_in, z < last, lower)
     for h in range(heads):
         qh, kh, vh, gh = q[:, hs(h)], k[:, hs(h)], v[:, hs(h)], grads[:, hs(h)]
         mixing = jnp.where(causal, mm(gh, vh, NT) * factor, 0.0).astype(BF)
         qg[:, hs(h)] = (mm(mixing, kh, NN) + mm(gh, prefix[h], NT) * factor).astype(BF)
         kg32[:, hs(h)] = mm(mixing, qh, TN)
         vg32[:, hs(h)] = mm(sc[h], gh, TN)
-
-    for i in range(1, nz - 1):
-        rs_round(i, False)
+    rs_round(2, False)
+    relay("suf", suf_out, t_own, t_sib, suf_in, suf_sib, z < last, z > 0, lower)
+    rs_round(3, False)
 
     joined(suf_in, suf_sib, t_sib, z < last, "suf", c == 0, prefix)
     for h in range(heads):
@@ -305,11 +326,18 @@
         kg[:, hs(h)] = (kg32[:, hs(h)] + mm(vh, prefix[h], NT) * factor).astype(BF)
         vg[:, hs(h)] = (vg32[:, hs(h)] + mm(kh, prefix[h], NN) * factor).astype(BF)
 
-    for j in range(2 * nz):
-        got(("mix", j), mix_in.at[j], xpart)
-        mixed[:, j * cols:(j + 1) * cols] = (
-            mix_out[j].astype(F32) + mix_in[j].astype(F32)
-        ).astype(BF)
+    for d in range(nz):
+        for way, ok, chip in (("up", z >= d, z - d), ("dn", z + d <= last, z + d)):
+            if d == 0 and way == "dn":
+                continue
+            for core, j in ((0, chip * 2 + c), (1, chip * 2 + o)):
+                @pl.when(ok)
+                def _():
+                    got(("mix", way, d, core), mix_in.at[j], xpart)
+                    jc = pl.ds(pl.multiple_of(j * cols, cols), cols)
+                    mixed[:, jc] = (
+                        mix_out[j].astype(F32) + mix_in[j].astype(F32)
+                    ).astype(BF)
 
     here = pl.ds(pl.multiple_of(z * cols, cols), cols)
     for r in range(CHUNKS):
@@ -331,6 +359,12 @@
                 make(name, src, dst, to).wait_send()
 
 
+def placed(*refs):
+    n = len(refs) // 2
+    for i in range(n):
+        refs[n + i][...] = refs[i][...]
+
+
 def fused(query_rows, key_rows, value_rows, out_weight, out_grad):
     length, width = query_rows.shape
     model = out_grad.shape[1]
@@ -340,7 +374,7 @@
     total = length * nseq
     heads = width // HD
     half = heads // 2
-    ids = message_ids(nz)
+    ids = message_ids(nz, half)
     state = (heads, HD, HD)
     hstate = (half, HD, HD)
     vm = pltpu.VMEM
@@ -358,7 +392,7 @@
     ]
     block = jax.ShapeDtypeStruct((length, width), BF)
     spec = pl.BlockSpec(memory_space=pltpu.VMEM)
-    return pl.pallas_call(
+    results = pl.pallas_call(
         functools.partial(
             kernel, nz, ids, 1.0 / math.sqrt(HD * total), 1.0 / math.sqrt(total)
         ),
@@ -373,6 +407,16 @@
             collective_id=0, has_side_effects=True, vmem_limit_bytes=52 * 2**20
         ),
     )(query_rows, key_rows, value_rows, out_weight, out_grad)
+    blocks = 4
+    specs = [pl.BlockSpec((a.shape[0] // blocks, a.shape[1]), lambda i: (i, 0)) for a in results]
+    return pl.pallas_call(
+        placed,
+        grid=(blocks,),
+        out_shape=tuple(jax.ShapeDtypeStruct(a.shape, a.dtype) for a in results),
+        in_specs=specs,
+        out_specs=tuple(specs),
+        compiler_params=pltpu.CompilerParams(vmem_limit_bytes=40 * 2**20),
+    )(*results)
 
 
 def prefix_2(value, axis, join, neutral, backward):
@@ -457,8 +501,8 @@
 def fits(mesh):
     shape = mesh.shape
     return (
-        shape["groups"] == 2 and shape["fsdp"] == 2 and shape["seq"] % 2 == 0
-        and 2 < shape["seq"] <= 8
+        shape["groups"] == 2 and shape["fsdp"] == 2
+        and shape["seq"] == 8
     )
 
 

time: 96.5 us -> 88.5 us (0.917); the launches traced: 94.8 us -> 88.3 us
  Pallas kernels: 88.5 us -> 85.2 us
  local copies, waits for them, and re-layouts: 5.66 us -> 2.44 us
    pallas_call x1, Pallas kernels: 88.5 us -> 82.9 us  [fused(): pl.pallas_call(functools.partial(kernel, nz, ids, 1.0 / math.sqrt(HD * to...]
    unnamed x7 -> x4, local copies, waits for them, and re-layouts: 5.66 us -> 2.44 us
    pallas_call x0 -> x1, Pallas kernels: none -> 2.25 us  [fused(): pl.pallas_call(placed, grid=(blocks,), out_shape=tuple((jax.ShapeDtypeStr...]
where the time goes in v2:
time: 88.5 us; the launch traced here: 88.3 us
  Pallas kernels  85.2 us (96%)
  local copies, waits for them, and re-layouts  2.44 us (3%)
    pallas_call x1, Pallas kernels, fused(): pl.pallas_call(functools.partial(kernel, nz, ids, 1.0 / math.sqrt(HD * to...  82.9 us
    unnamed x4, local copies, waits for them, and re-layouts  2.44 us
    pallas_call x1, Pallas kernels, fused(): pl.pallas_call(placed, grid=(blocks,), out_shape=tuple((jax.ShapeDtypeStr...  2.25 us

profile of v2, /device:TPU:0, one launch (start us, length us, event | category | flops | bytes accessed | tf_op | source)
XLA Modules:
  0.0 88.3 jit_solution(2814232980519021091)
XLA Ops:
  0.6 82.9 %shard_map.92 = (bf16[256,2048]{1,0:T(8,128)(2,1)}, bf16[256,1024]{1,0:T(8,128)(2,1)S(1)}, bf16[256,1024]{1,0:T(8,128)(2,1)S(1)}, bf16[256,1024]{1,0:T(8,128)(2,1)S(1)}, f32[1024,256]{1,0:T(8,128)}) custom-call(bf16[256,1024]{1,0:T(8,128)(2,1)} %q.1, bf16[256,1024]{1,0:T(8,128)(2,1)} %k.1, bf16[256,1024]{1,0:T(8,128)(2,1)} %v.1, bf16[1024,256]{1,0:T(8,128)(2,1)} %w.1, ...), custom_call_target="tpu_custom_call" | custom-call | tf_op jit(solution)/shard_map/pallas_call | solution.py:395
  83.6 0.0 copy-start
  83.6 1.2 %copy-done = bf16[256,2048]{1,0:T(8,128)(2,1)S(1)} copy-done((bf16[256,2048]{1,0:T(8,128)(2,1)S(1)}, bf16[256,2048]{1,0:T(8,128)(2,1)}, u32[]{:S(2)}) %copy-start) | copy-done | bytes 1048600
  84.8 0.0 copy-start.1
  84.8 1.2 %copy-done.1 = f32[1024,256]{1,0:T(8,128)S(1)} copy-done((f32[1024,256]{1,0:T(8,128)S(1)}, f32[1024,256]{1,0:T(8,128)}, u32[]{:S(2)}) %copy-start.1) | copy-done | bytes 1048600
  86.0 2.3 %shard_map.93 = (bf16[256,2048]{1,0:T(8,128)(2,1)}, bf16[256,1024]{1,0:T(8,128)(2,1)}, bf16[256,1024]{1,0:T(8,128)(2,1)}, bf16[256,1024]{1,0:T(8,128)(2,1)}, f32[1024,256]{1,0:T(8,128)}) custom-call(bf16[256,2048]{1,0:T(8,128)(2,1)S(1)} %copy-done, bf16[256,1024]{1,0:T(8,128)(2,1)S(1)} %get-tuple-element.11.refs_1_, ...), custom_call_target="tpu_custom_call" | custom-call | tf_op jit(solution)/shard_map/pallas_call | solution.py:412
Async XLA Ops:
  83.6 1.2 %copy-start = (bf16[256,2048]{1,0:T(8,128)(2,1)S(1)}, bf16[256,2048]{1,0:T(8,128)(2,1)}, u32[]{:S(2)}) copy-start(bf16[256,2048]{1,0:T(8,128)(2,1)} %get-tuple-element.10.refs_0_) | copy-start | bytes 3145732
  84.8 1.2 %copy-start.1 = (f32[1024,256]{1,0:T(8,128)S(1)}, f32[1024,256]{1,0:T(8,128)}, u32[]{:S(2)}) copy-start(f32[1024,256]{1,0:T(8,128)} %get-tuple-element.14.refs_4_) | copy-start | bytes 3145732
